TPU v7x, 32 devices: a whole 2x2x4 slice. The times are simulated.
32 devices in a mesh: parts: 2 (over y), track: 4 (over z), tm: 2 (over x), coef: 2 (over core).
Axes of the slice: x: 2, y: 2, z: 4, core: 2. Of those that a mesh axis runs over, the one named last changes fastest.
Arguments:
- sector_ids: int32 [12288], P(('parts', 'track', 'tm')), parts along dimension 0, may hold values from 0 to 63, as said below
- observed: float32 [3, 12288], P(None, ('parts', 'track', 'tm')), parts along dimension 1, may hold values from -6 to 6
- weights: float32 [3, 12288], P(None, ('parts', 'track', 'tm')), parts along dimension 1, may hold values from 0.3 to 3
- coefficients: float32 [2048, 128], P(('parts', 'track')), parts along dimension 0, may hold values from -6 to 6
- tile_index: int32 [128, 12], P(('parts', 'track', 'tm'), 'coef'), parts along dimension 0, may hold values from 0 to 1023, as said below
- tile_count: int32 [128], P(('parts', 'track', 'tm')), parts along dimension 0, may hold values from 3 to 12
- sensitivity: bfloat16 [128, 12, 3, 128, 128], P(('parts', 'track', 'tm'), 'coef'), parts along dimension 0, may hold values from -0.15625 to 0.15625
Outputs:
- gradient: float32 [2048, 128], P(('parts', 'track')), parts along dimension 0
There are 2 independent parts, one for each index of `parts`. A program takes and returns all parts, laid end to end along the dimension named above; each array names one. Nothing has to cross between parts.
Inputs may be any that keep to these rules, and one draw needn't show every extreme that they name: `sector_ids`: the rows of one index of track and tm fall in at most 192 rows into the 8 consecutive sectors of any one index, and some pair reaches 192; the sectors of each index receive exactly 768 rows in all; each sector holds at most 128 rows, and every index holds a sector with exactly 128. `tile_index`: entries at positions from tile_count on are arbitrary blocks and take no part. Block n belongs to track index n // 256. Of the 48 entries held by one index of track, tm and coef (its sectors' rows, its coef share of the columns), live or not, at most 24 name blocks of any one track index, and every such device has a track index named exactly 24 times.
All inputs are finite; a program needn't handle non-finite values.
Results may differ from a plain program's by a relative error of at most 0.0037.
Values may be sent and summed in bfloat16 or wider, within the bound.
A program may use at most 64 MiB of HBM per device.

v0:
```python
import jax
import jax.numpy as jnp
from jax import lax
from jax.sharding import PartitionSpec as P

HUBER = 2.0


def per_device(sector_ids, observed, weights, coefficients, tile_index, tile_count, sensitivity):
    sector_total = tile_index.shape[0]
    half_k = tile_index.shape[1]
    slot_count = sensitivity.shape[3]
    block_width = sensitivity.shape[4]
    owners = lax.axis_size(("track", "tm"))
    row_total = sector_ids.shape[0]
    capacity = 2 * row_total // owners
    rounded = coefficients.astype(jnp.bfloat16)
    every_block = lax.all_gather(rounded, "track", axis=0, tiled=True)
    owner_of = sector_ids // sector_total
    local_sector = sector_ids % sector_total
    onehot = (owner_of[:, None] == jnp.arange(owners, dtype=jnp.int32)[None, :]).astype(jnp.int32)
    ranking = jnp.sum((jnp.cumsum(onehot, axis=0) - 1) * onehot, axis=1)
    placing = owner_of * capacity + ranking
    payload = jnp.concatenate([observed, weights], axis=0)
    outgoing = jnp.zeros((6, owners * capacity), jnp.float32).at[:, placing].set(payload)
    outgoing = jnp.transpose(outgoing.reshape(6, owners, capacity), (1, 0, 2))
    labels = jnp.full((owners * capacity,), -1, jnp.int32).at[placing].set(local_sector)
    labels = labels.reshape(owners, capacity)
    got_rows, got_labels = (
        lax.all_to_all(outgoing, ("track", "tm"), split_axis=0, concat_axis=0, tiled=True),
        lax.all_to_all(labels, ("track", "tm"), split_axis=0, concat_axis=0, tiled=True),
    )
    received = jnp.transpose(got_rows, (1, 0, 2)).reshape(6, owners * capacity)
    flat_labels = got_labels.reshape(owners * capacity)
    member = (flat_labels[:, None] == jnp.arange(sector_total, dtype=jnp.int32)[None, :]).astype(
        jnp.int32
    )
    within = jnp.sum((jnp.cumsum(member, axis=0) - 1) * member, axis=1)
    target = jnp.where(
        flat_labels >= 0, flat_labels * slot_count + within, sector_total * slot_count
    )
    gridded = jnp.zeros((6, sector_total * slot_count + 1), jnp.float32).at[:, target].set(received)
    gridded = jnp.transpose(gridded[:, :-1].reshape(6, sector_total, slot_count), (1, 0, 2))
    observed_tiles = gridded[:, :3]
    weight_tiles = gridded[:, 3:]
    k_global = lax.axis_index("coef") * half_k + jnp.arange(half_k, dtype=jnp.int32)
    active = k_global[None, :] < tile_count[:, None]
    blocks = jnp.take(every_block, tile_index, axis=0)
    blocks = jnp.where(active[:, :, None], blocks, jnp.zeros_like(blocks))
    partial_pred = jnp.einsum(
        "skcjb,skb->scj", sensitivity, blocks, preferred_element_type=jnp.float32
    )
    predicted = lax.psum(partial_pred, "coef")
    scaled = weight_tiles * (predicted - observed_tiles)
    force = (weight_tiles * scaled / jnp.sqrt(1.0 + (scaled / HUBER) ** 2)).astype(jnp.bfloat16)
    tile_grad = jnp.einsum("skcjb,scj->skb", sensitivity, force, preferred_element_type=jnp.float32)
    tile_grad = jnp.where(active[:, :, None], tile_grad, jnp.zeros_like(tile_grad))
    block_total = every_block.shape[0]
    partial_grad = jnp.zeros((block_total, block_width), jnp.float32)
    partial_grad = partial_grad.at[tile_index.reshape(-1)].add(tile_grad.reshape(-1, block_width))
    summed = lax.psum_scatter(partial_grad, "track", scatter_dimension=0, tiled=True)
    gradient = lax.psum(summed, ("tm", "coef"))
    return gradient


def solution(mesh):
    placed = (
        P(("parts", "track", "tm")),
        P(None, ("parts", "track", "tm")),
        P(None, ("parts", "track", "tm")),
        P(("parts", "track"), None),
        P(("parts", "track", "tm"), "coef"),
        P(("parts", "track", "tm")),
        P(("parts", "track", "tm"), "coef", None, None, None),
    )
    return jax.shard_map(
        per_device,
        mesh=mesh,
        in_specs=placed,
        out_specs=P(("parts", "track"), None),
        check_vma=False,
    )
```

profile of v0, /device:TPU:0, one launch (start us, length us, event | category | flops | bytes accessed | tf_op | source)
XLA Modules:
  0.0 135.0 jit_solution(9949122944024813271)
XLA Ops:
  6.5 0.7 add_select_fusion
  7.2 1.7 %reduce-window.14 = s32[8,6,128]{2,0,1:T(8,128)S(1)} reduce-window(s32[8,6,128]{2,0,1:T(8,128)S(1)} %fusion.13, s32[]{:T(128)} %constant.40.clone.1), window={size=1x1x128 pad=0_0x0_0x127_0}, to_apply=%region_0.1 | reduce-window | flops 780288 | bytes 49156 | tf_op jit(solution)/shard_map/reduce-window
  8.9 0.1 slice.30
  9.0 0.1 copy.24
  9.2 0.2 reduce-window.15
  9.3 0.1 copy.25
  9.4 0.1 fusion.11
  9.5 3.4 %scatter_custom_fusion = s32[1536]{0:T(1024)S(1)} fusion(s32[768]{0:T(1024)S(1)} %compare_select_fusion.2, s32[768]{0:T(1024)S(1)} %get-tuple-element.7, s32[]{:T(128)} %constant.74.clone.1), kind=kCustom, calls=%fused_computation.50 | custom fusion | bytes 6148 | tf_op jit(solution)/shard_map/scatter | solution.py:27
  12.9 0.7 all_to_all.9
  13.6 7.3 %all-to-all-start = ((s32[8,1,192]{2,1,0:T(1,128)}), s32[8,1,192]{2,1,0:T(1,128)S(1)}, u32[]{:S(2)}, u32[]{:S(2)}) async-start(s32[8,1,192]{2,1,0:T(1,128)} %all_to_all.9), calls=%async_computation | async-start | bytes 16384 | tf_op jit(solution)/shard_map/all_to_all | solution.py:31
  20.8 0.7 compare_select_fusion.1
  21.5 0.8 reshape.166
  22.3 0.7 maximum_bitcast_fusion
  23.0 0.2 copy.26
  23.2 4.4 %scatter_custom_fusion.1 = f32[6,1536]{0,1:T(8,128)S(1)} fusion(s32[768]{0:T(1024)S(1)} %compare_select_fusion.2, f32[768,6]{1,0:T(8,128)S(1)} %copy.26, f32[]{:T(128)} %constant.39.clone.1), kind=kCustom, calls=%fused_computation.7 | custom fusion | bytes 36868 | tf_op jit(solution)/shard_map/scatter | solution.py:25
  27.6 1.0 copy.27
  28.6 0.9 convert_element_type.18
  29.5 14.5 %all_gather.3 = bf16[1024,128]{1,0:T(8,128)(2,1)S(1)} all-gather(bf16[256,128]{1,0:T(8,128)(2,1)S(1)} %convert_element_type.18), channel_id=1, replica_groups=mesh['parts'=2,'track'=4,'tm'=2,'coef'=2] {'track'}, dimensions={0}, use_global_device_ids=true | all-gather | bytes 327680 | tf_op jit(solution)/shard_map/all_gather | solution.py:18
  44.0 0.1 reshape.175
  44.0 0.6 gather_fusion
  44.7 0.8 compare_and_fusion
  45.4 0.1 select_bitcast_fusion
  45.5 3.7 %fusion = f32[8,1,3,128,1]{3,1,4,2,0:T(1,128)S(1)} fusion(bf16[8,6,3,128,128]{4,3,2,1,0:T(8,128)(2,1)} %param.13, bf16[8,6,128,1,1]{2,1,0,3,4:T(8,128)(2,1)S(1)} %select_bitcast_fusion), kind=kOutput, calls=%fused_computation.5 | convolution fusion | flops 4718592 | bytes 4743168 | tf_op jit(solution)/shard_map/skcjb,skb->scj/dot_general | solution.py:50
  49.2 3.3 %psum.14 = f32[8,3,128]{2,0,1:T(8,128)S(1)} all-reduce(f32[8,3,128]{2,0,1:T(8,128)S(1)} %bitcast.50), channel_id=1, replica_groups=mesh['parts'=2,'track'=4,'tm'=2,'coef'=2] {'coef'}, use_global_device_ids=true, to_apply=%region_9.10 | all-reduce | flops 3072 | bytes 24576 | tf_op jit(solution)/shard_map/psum | solution.py:53
  52.5 5.7 %all-to-all-start.1 = ((f32[8,6,192]{2,1,0:T(8,128)}), f32[8,6,192]{2,1,0:T(8,128)S(1)}, u32[]{:S(2)}, u32[]{:S(2)}) async-start(f32[8,6,192]{2,1,0:T(8,128)} %bitcast.8), calls=%async_computation.1 | async-start | bytes 131072 | tf_op jit(solution)/shard_map/all_to_all | solution.py:30
  58.2 0.0 reduce-scatter.2.cloned.1.call-start
  58.3 0.1 eq.61
  58.4 0.1 eq.57
  58.5 2.3 %reduce-window.16 = s32[8,12,128]{2,1,0:T(8,128)S(1)} reduce-window(s32[8,12,128]{2,1,0:T(8,128)S(1)} %fusion.8, s32[]{:T(128)} %constant.40.clone.1), window={size=1x1x128 pad=0_0x0_0x127_0}, to_apply=%region_4.5 | reduce-window | flops 1560576 | bytes 98308 | tf_op jit(solution)/shard_map/reduce-window.2
  60.7 0.3 slice_reduce_fusion
  61.0 0.2 reduce-window.19
  61.2 0.1 add_bitcast_fusion
  61.3 0.1 mul.43
  61.4 0.1 ge.21
  61.6 3.5 %all-to-all-done.1 = f32[8,6,192]{2,1,0:T(8,128)S(1)} async-done(((f32[8,6,192]{2,1,0:T(8,128)}), f32[8,6,192]{2,1,0:T(8,128)S(1)}, u32[]{:S(2)}, u32[]{:S(2)}) %all-to-all-start.1) | async-done | bytes 36896 | tf_op jit(solution)/shard_map/all_to_all | solution.py:30
  65.1 0.1 reshape.198
  65.2 0.3 copy.29
  65.5 4.4 %scatter_custom_fusion.2 = f32[6,1025]{0,1:T(8,128)S(1)} fusion(s32[1536]{0:T(1024)S(1)} %fusion.17, f32[1536,6]{1,0:T(8,128)S(1)} %copy.29, f32[]{:T(128)} %constant.39.clone.1), kind=kCustom, calls=%fused_computation.9 | custom fusion | bytes 24604 | tf_op jit(solution)/shard_map/scatter | solution.py:42
  70.0 0.2 copy.36
  70.2 3.1 %fusion.15 = f32[8,1,6,128,1]{3,1,4,2,0:T(1,128)S(1)} fusion(bf16[8,6,3,128,128]{4,3,2,1,0:T(8,128)(2,1)} %param.13, bf16[8,3,128,1,1]{2,0,1,3,4:T(8,128)(2,1)S(1)} %fusion.18), kind=kOutput, calls=%fused_computation.34 | convolution fusion | flops 4718592 | bytes 4749312 | tf_op jit(solution)/shard_map/skcjb,scj->skb/dot_general | solution.py:56
  73.3 0.1 bitcast_select_fusion
  73.4 1.5 %scatter_custom_fusion.3 = f32[1024,128]{1,0:T(8,128)} fusion(s32[48]{0:T(128)S(1)} %fusion.23, f32[48,128]{1,0:T(8,128)S(1)} %reshape.209, f32[]{:T(128)} %constant.39.clone.1), kind=kCustom, calls=%fused_computation.11 | custom fusion | flops 6144 | bytes 524292 | tf_op jit(solution)/shard_map/scatter-add | solution.py:60
  74.9 0.0 reduce-scatter.2.cloned.1.call-update
  75.0 0.0 all-reduce.2.cloned.1.call-start
  75.0 19.6 %reduce-scatter.2.cloned.1.call-done = f32[256,128]{1,0:T(8,128)} async-done(((f32[1024,128]{1,0:T(8,128)}), f32[256,128]{1,0:T(8,128)}) %reduce-scatter.2.cloned.1.call-update) | async-done | bytes 131088 | tf_op jit(solution)/shard_map/reduce_scatter | solution.py:61
  94.6 0.0 all-reduce.2.cloned.1.call-update
  94.7 32.0 %all-reduce.2.cloned.1.call-done = f32[256,128]{1,0:T(8,128)} async-done(((f32[256,128]{1,0:T(8,128)}), f32[256,128]{1,0:T(8,128)}) %all-reduce.2.cloned.1.call-update) | async-done | bytes 131088 | tf_op jit(solution)/shard_map/psum | solution.py:62
  126.6 1.6 %copy.49 = f32[256,128]{1,0:T(8,128)} copy(f32[256,128]{1,0:T(8,128)} %all-reduce.2.cloned.1.call-done) | data formatting | bytes 262144
  (17 shorter events, 0.3 us)
Async XLA Ops:
  13.6 38.9 %all-to-all-start = ((s32[8,1,192]{2,1,0:T(1,128)}), s32[8,1,192]{2,1,0:T(1,128)S(1)}, u32[]{:S(2)}, u32[]{:S(2)}) async-start(s32[8,1,192]{2,1,0:T(1,128)} %all_to_all.9), calls=%async_computation | async-start | bytes 16384 | tf_op jit(solution)/shard_map/all_to_all | solution.py:31
  52.5 12.6 %all-to-all-start.1 = ((f32[8,6,192]{2,1,0:T(8,128)}), f32[8,6,192]{2,1,0:T(8,128)S(1)}, u32[]{:S(2)}, u32[]{:S(2)}) async-start(f32[8,6,192]{2,1,0:T(8,128)} %bitcast.8), calls=%async_computation.1 | async-start | bytes 131072 | tf_op jit(solution)/shard_map/all_to_all | solution.py:30
  58.2 36.4 %reduce-scatter.2.cloned.1.call-start = ((), (), s32[]{:S(2)}) async-start(), calls=%async_computation.3 | async-start | bytes 655360 | tf_op jit(solution)/shard_map/reduce_scatter | solution.py:61
  75.0 51.7 %all-reduce.2.cloned.1.call-start = ((), (), s32[]{:S(2)}) async-start(), calls=%async_computation.4 | async-start | bytes 262144 | tf_op jit(solution)/shard_map/psum | solution.py:62
Sparse Core Ops, SparseCore 0:
  75.1 19.5 reduce-scatter.1
  97.0 29.6 all-reduce.1
where the time goes:
time: 136 us; the launch traced here: 135 us
  waiting for transfers between devices  55.2 us (41%)
  local copies, waits for them, and re-layouts  18.6 us (14%)
  blocking collectives  17.8 us (13%)
  between operations  13.5 us (10%)
  starting transfers between devices  13.1 us (10%)
  other arithmetic  10.2 us (7%)
  matrix products  6.73 us (5%)
    psum x1, waiting for transfers between devices, per_device(): gradient = lax.psum(summed, ('tm', 'coef'))  32 us
    reduce_scatter x1, waiting for transfers between devices, per_device(): lax.psum_scatter(partial_grad, 'track', scatter_dimension=0, tiled=True)  19.6 us
    all_gather x1, blocking collectives, per_device(): every_block = lax.all_gather(rounded, 'track', axis=0, tiled=True)  14.5 us
    all_to_all x1, starting transfers between devices, per_device(): lax.all_to_all(labels, ('track', 'tm'), split_axis=0, concat_axis=0, tile...  7.25 us
    all_to_all x1, starting transfers between devices, per_device(): lax.all_to_all(outgoing, ('track', 'tm'), split_axis=0, concat_axis=0, ti...  5.72 us
    scatter x1, local copies, waits for them, and re-layouts, per_device(): jnp.zeros((6, sector_total * slot_count + 1), jnp.float32).at[:, target]  4.45 us
    scatter x1, local copies, waits for them, and re-layouts, per_device(): jnp.zeros((6, owners * capacity), jnp.float32).at[:, placing].set(payload)  4.36 us
    another operation x4, other arithmetic  4.31 us
  transfers between devices with their start and end apart: 4, of which 3 were waited for; matrix products, arithmetic and copies ran while one was open for 13% of the time, Pallas kernels for 0%

commit v1 on v0

--- a/solution.py
+++ b/solution.py
@@ -15,7 +15,14 @@
     row_total = sector_ids.shape[0]
     capacity = 2 * row_total // owners
     rounded = coefficients.astype(jnp.bfloat16)
-    every_block = lax.all_gather(rounded, "track", axis=0, tiled=True)
+    ring = [rounded]
+    for hop in range(3):
+        ring.append(lax.ppermute(ring[-1], "track", [(dev, (dev + 1) % 4) for dev in range(4)]))
+    every_block = jnp.roll(
+        jnp.concatenate(ring[::-1], axis=0),
+        (lax.axis_index("track") + 1) * ring[0].shape[0],
+        axis=0,
+    )
     owner_of = sector_ids // sector_total
     local_sector = sector_ids % sector_total
     onehot = (owner_of[:, None] == jnp.arange(owners, dtype=jnp.int32)[None, :]).astype(jnp.int32)

time: 136 us -> 129 us (0.949)
  blocking collectives: 17.8 us -> 3.3 us
  waiting for transfers between devices: 55.2 us -> 59.6 us
  starting transfers between devices: 13.1 us -> 16.1 us
    all_gather x1 -> x0, blocking collectives: 14.5 us -> none  [per_device(): every_block = lax.all_gather(rounded, 'track', axis=0, tiled=True)]
    ppermute x0 -> x3, starting transfers between devices: none -> 5.22 us  [per_device(): lax.ppermute(ring[-1], 'track', [(dev, (dev + 1) % 4) for dev in range(4)])]
    ppermute x0 -> x3, waiting for transfers between devices: none -> 4.8 us  [per_device(): lax.ppermute(ring[-1], 'track', [(dev, (dev + 1) % 4) for dev in range(4)])]
    all_to_all x1, waiting for transfers between devices: 3.54 us -> 0.01 us  [per_device(): lax.all_to_all(outgoing, ('track', 'tm'), split_axis=0, concat_axis=0, ti...]
    reduce_scatter x1, waiting for transfers between devices: 19.6 us -> 22.8 us  [per_device(): lax.psum_scatter(partial_grad, 'track', scatter_dimension=0, tiled=True)]
    all_to_all x1, starting transfers between devices: 7.25 us -> 4.79 us  [per_device(): lax.all_to_all(labels, ('track', 'tm'), split_axis=0, concat_axis=0, tile...]
  transfers between devices with their start and end apart: 4 -> 7, of which waited for: 3 -> 4; matrix products, arithmetic and copies ran while one was open for 13% -> 18% of each run, Pallas kernels for 0% -> 0%
where the time goes in v1:
time: 129 us; the launch traced here: 128 us
  waiting for transfers between devices  59.6 us (46%)
  local copies, waits for them, and re-layouts  18.7 us (14%)
  starting transfers between devices  16.1 us (12%)
  between operations  13.6 us (11%)
  other arithmetic  10.3 us (8%)
  matrix products  6.73 us (5%)
  blocking collectives  3.3 us (3%)
    psum x1, waiting for transfers between devices, per_device(): gradient = lax.psum(summed, ('tm', 'coef'))  31.9 us
    reduce_scatter x1, waiting for transfers between devices, per_device(): lax.psum_scatter(partial_grad, 'track', scatter_dimension=0, tiled=True)  22.8 us
    all_to_all x1, starting transfers between devices, per_device(): lax.all_to_all(outgoing, ('track', 'tm'), split_axis=0, concat_axis=0, ti...  6 us
    ppermute x3, starting transfers between devices, per_device(): lax.ppermute(ring[-1], 'track', [(dev, (dev + 1) % 4) for dev in range(4)])  5.22 us
    ppermute x3, waiting for transfers between devices, per_device(): lax.ppermute(ring[-1], 'track', [(dev, (dev + 1) % 4) for dev in range(4)])  4.8 us
    all_to_all x1, starting transfers between devices, per_device(): lax.all_to_all(labels, ('track', 'tm'), split_axis=0, concat_axis=0, tile...  4.79 us
    scatter x1, local copies, waits for them, and re-layouts, per_device(): jnp.zeros((6, sector_total * slot_count + 1), jnp.float32).at[:, target]  4.45 us
    scatter x1, local copies, waits for them, and re-layouts, per_device(): jnp.zeros((6, owners * capacity), jnp.float32).at[:, placing].set(payload)  4.36 us
  transfers between devices with their start and end apart: 7, of which 4 were waited for; matrix products, arithmetic and copies ran while one was open for 18% of the time, Pallas kernels for 0%

profile of v1, /device:TPU:0, one launch (start us, length us, event | category | flops | bytes accessed | tf_op | source)
XLA Modules:
  0.0 128.3 jit_solution(11754154313145519327)
XLA Ops:
  6.5 1.0 convert_element_type.18
  7.5 3.0 %collective-permute-start = (bf16[256,128]{1,0:T(8,128)(2,1)S(1)}, bf16[256,128]{1,0:T(8,128)(2,1)S(1)}, u32[]{:S(2)}, u32[]{:S(2)}) collective-permute-start(bf16[256,128]{1,0:T(8,128)(2,1)S(1)} %convert_element_type.18), channel_id=1, source_target_pairs={{0,4},{4,8},{8,12},{12,0},{1,5},{5,9},{9,13},{13,1},{2,6},{6,10},{... | collective-permute-start | bytes 196616 | tf_op jit(solution)/shard_map/ppermute | solution.py:20
  10.5 0.7 add_select_fusion
  11.2 1.7 %reduce-window.14 = s32[8,6,128]{2,0,1:T(8,128)S(1)} reduce-window(s32[8,6,128]{2,0,1:T(8,128)S(1)} %fusion.13, s32[]{:T(128)} %constant.93.clone.1), window={size=1x1x128 pad=0_0x0_0x127_0}, to_apply=%region_0.1 | reduce-window | flops 780288 | bytes 49156 | tf_op jit(solution)/shard_map/reduce-window
  13.0 0.1 slice.30
  13.0 0.1 copy.24
  13.2 0.2 reduce-window.15
  13.3 0.1 copy.25
  13.4 0.1 fusion.11
  13.5 3.4 %scatter_custom_fusion = s32[1536]{0:T(1024)S(1)} fusion(s32[768]{0:T(1024)S(1)} %compare_select_fusion.2, s32[768]{0:T(1024)S(1)} %get-tuple-element.7, s32[]{:T(128)} %constant.97.clone.1), kind=kCustom, calls=%fused_computation.58 | custom fusion | bytes 6148 | tf_op jit(solution)/shard_map/scatter | solution.py:34
  16.9 0.7 all_to_all.9
  17.6 4.8 %all-to-all-start = ((s32[8,1,192]{2,1,0:T(1,128)}), s32[8,1,192]{2,1,0:T(1,128)S(1)}, u32[]{:S(2)}, u32[]{:S(2)}) async-start(s32[8,1,192]{2,1,0:T(1,128)} %all_to_all.9), calls=%async_computation | async-start | bytes 16384 | tf_op jit(solution)/shard_map/all_to_all | solution.py:38
  22.4 0.7 compare_select_fusion.1
  23.1 0.8 reshape.166
  23.8 0.1 reshape.175
  23.9 0.8 compare_and_fusion
  24.7 0.7 maximum_bitcast_fusion
  25.5 0.2 copy.26
  25.7 4.4 %scatter_custom_fusion.1 = f32[6,1536]{0,1:T(8,128)S(1)} fusion(s32[768]{0:T(1024)S(1)} %compare_select_fusion.2, f32[768,6]{1,0:T(8,128)S(1)} %copy.26, f32[]{:T(128)} %constant.92.clone.1), kind=kCustom, calls=%fused_computation.7 | custom fusion | bytes 36868 | tf_op jit(solution)/shard_map/scatter | solution.py:32
  30.0 1.0 copy.27
  31.0 6.0 %all-to-all-start.1 = ((f32[8,6,192]{2,1,0:T(8,128)}), f32[8,6,192]{2,1,0:T(8,128)S(1)}, u32[]{:S(2)}, u32[]{:S(2)}) async-start(f32[8,6,192]{2,1,0:T(8,128)} %bitcast.8), calls=%async_computation.1 | async-start | bytes 131072 | tf_op jit(solution)/shard_map/all_to_all | solution.py:37
  37.1 0.1 eq.64
  37.2 0.1 eq.60
  37.2 2.3 %reduce-window.16 = s32[8,12,128]{2,1,0:T(8,128)S(1)} reduce-window(s32[8,12,128]{2,1,0:T(8,128)S(1)} %fusion.8, s32[]{:T(128)} %constant.93.clone.1), window={size=1x1x128 pad=0_0x0_0x127_0}, to_apply=%region_4.5 | reduce-window | flops 1560576 | bytes 98308 | tf_op jit(solution)/shard_map/reduce-window.2
  39.5 0.3 slice_reduce_fusion
  39.8 0.2 reduce-window.19
  40.0 0.1 add_bitcast_fusion
  40.1 0.1 mul.46
  40.2 0.1 ge.21
  40.3 2.0 %collective-permute-start.1 = (bf16[256,128]{1,0:T(8,128)(2,1)S(1)}, bf16[256,128]{1,0:T(8,128)(2,1)S(1)}, u32[]{:S(2)}, u32[]{:S(2)}) collective-permute-start(bf16[256,128]{1,0:T(8,128)(2,1)S(1)} %collective-permute-done), channel_id=1, source_target_pairs={{0,4},{4,8},{8,12},{12,0},{1,5},{5,9},{9,13},{13,1},{2,6},{6,10},{... | collective-permute-start | bytes 196616 | tf_op jit(solution)/shard_map/ppermute | solution.py:20
  42.3 4.1 %collective-permute-done.1 = bf16[256,128]{1,0:T(8,128)(2,1)S(1)} collective-permute-done((bf16[256,128]{1,0:T(8,128)(2,1)S(1)}, bf16[256,128]{1,0:T(8,128)(2,1)S(1)}, u32[]{:S(2)}, u32[]{:S(2)}) %collective-permute-start.1) | collective-permute-done | bytes 65568 | tf_op jit(solution)/shard_map/ppermute | solution.py:20
  46.4 0.2 collective-permute-start.2
  46.6 0.1 reshape.198
  46.7 0.3 copy.29
  47.0 4.4 %scatter_custom_fusion.2 = f32[6,1025]{0,1:T(8,128)S(1)} fusion(s32[1536]{0:T(1024)S(1)} %fusion.17, f32[1536,6]{1,0:T(8,128)S(1)} %copy.29, f32[]{:T(128)} %constant.92.clone.1), kind=kCustom, calls=%fused_computation.9 | custom fusion | bytes 24604 | tf_op jit(solution)/shard_map/scatter | solution.py:49
  51.5 0.2 copy.36
  51.7 0.7 collective-permute-done.2
  52.6 0.6 gather_fusion
  53.3 0.1 select_bitcast_fusion
  53.4 3.7 %fusion = f32[8,1,3,128,1]{3,1,4,2,0:T(1,128)S(1)} fusion(bf16[8,6,3,128,128]{4,3,2,1,0:T(8,128)(2,1)} %param.13, bf16[8,6,128,1,1]{2,1,0,3,4:T(8,128)(2,1)S(1)} %select_bitcast_fusion), kind=kOutput, calls=%fused_computation.5 | convolution fusion | flops 4718592 | bytes 4743168 | tf_op jit(solution)/shard_map/skcjb,skb->scj/dot_general | solution.py:57
  57.0 3.3 %psum.14 = f32[8,3,128]{2,0,1:T(8,128)S(1)} all-reduce(f32[8,3,128]{2,0,1:T(8,128)S(1)} %bitcast.50), channel_id=1, replica_groups=mesh['parts'=2,'track'=4,'tm'=2,'coef'=2] {'coef'}, use_global_device_ids=true, to_apply=%region_9.10 | all-reduce | flops 3072 | bytes 24576 | tf_op jit(solution)/shard_map/psum | solution.py:60
  60.3 3.1 %fusion.15 = f32[8,1,6,128,1]{3,1,4,2,0:T(1,128)S(1)} fusion(bf16[8,6,3,128,128]{4,3,2,1,0:T(8,128)(2,1)} %param.13, bf16[8,3,128,1,1]{2,0,1,3,4:T(8,128)(2,1)S(1)} %fusion.18), kind=kOutput, calls=%fused_computation.42 | convolution fusion | flops 4718592 | bytes 4749312 | tf_op jit(solution)/shard_map/skcjb,scj->skb/dot_general | solution.py:63
  63.4 0.1 bitcast_select_fusion
  63.5 1.5 %scatter_custom_fusion.3 = f32[1024,128]{1,0:T(8,128)} fusion(s32[48]{0:T(128)S(1)} %fusion.23, f32[48,128]{1,0:T(8,128)S(1)} %reshape.209, f32[]{:T(128)} %constant.92.clone.1), kind=kCustom, calls=%fused_computation.11 | custom fusion | flops 6144 | bytes 524292 | tf_op jit(solution)/shard_map/scatter-add | solution.py:67
  65.1 0.0 all-reduce.2.cloned.1.call-start
  65.1 22.8 %reduce-scatter.2.cloned.1.call-done = f32[256,128]{1,0:T(8,128)} async-done(((f32[1024,128]{1,0:T(8,128)}), f32[256,128]{1,0:T(8,128)}) %reduce-scatter.2.cloned.1.call-update) | async-done | bytes 131088 | tf_op jit(solution)/shard_map/reduce_scatter | solution.py:68
  88.0 31.9 %all-reduce.2.cloned.1.call-done = f32[256,128]{1,0:T(8,128)} async-done(((f32[256,128]{1,0:T(8,128)}), f32[256,128]{1,0:T(8,128)}) %all-reduce.2.cloned.1.call-update) | async-done | bytes 131088 | tf_op jit(solution)/shard_map/psum | solution.py:69
  119.9 1.6 %copy.56 = f32[256,128]{1,0:T(8,128)} copy(f32[256,128]{1,0:T(8,128)} %all-reduce.2.cloned.1.call-done) | data formatting | bytes 262144
  (33 shorter events, 0.5 us)
Async XLA Ops:
  6.5 46.0 %copy-start = (f32[256,128]{1,0:T(8,128)S(1)}, f32[256,128]{1,0:T(8,128)}, u32[]{:S(2)}) copy-start(f32[256,128]{1,0:T(8,128)} %param.10) | copy-start | bytes 393220
  7.5 32.8 %collective-permute-start = (bf16[256,128]{1,0:T(8,128)(2,1)S(1)}, bf16[256,128]{1,0:T(8,128)(2,1)S(1)}, u32[]{:S(2)}, u32[]{:S(2)}) collective-permute-start(bf16[256,128]{1,0:T(8,128)(2,1)S(1)} %convert_element_type.18), channel_id=1, source_target_pairs={{0,4},{4,8},{8,12},{12,0},{1,5},{5,9},{9,13},{13,1},{2,6},{6,10},{... | collective-permute-start | bytes 196616 | tf_op jit(solution)/shard_map/ppermute | solution.py:20
  17.6 13.4 %all-to-all-start = ((s32[8,1,192]{2,1,0:T(1,128)}), s32[8,1,192]{2,1,0:T(1,128)S(1)}, u32[]{:S(2)}, u32[]{:S(2)}) async-start(s32[8,1,192]{2,1,0:T(1,128)} %all_to_all.9), calls=%async_computation | async-start | bytes 16384 | tf_op jit(solution)/shard_map/all_to_all | solution.py:38
  31.0 15.6 %all-to-all-start.1 = ((f32[8,6,192]{2,1,0:T(8,128)}), f32[8,6,192]{2,1,0:T(8,128)S(1)}, u32[]{:S(2)}, u32[]{:S(2)}) async-start(f32[8,6,192]{2,1,0:T(8,128)} %bitcast.8), calls=%async_computation.1 | async-start | bytes 131072 | tf_op jit(solution)/shard_map/all_to_all | solution.py:37
  37.0 50.9 %reduce-scatter.2.cloned.1.call-start = ((), (), s32[]{:S(2)}) async-start(), calls=%async_computation.3 | async-start | bytes 655360 | tf_op jit(solution)/shard_map/reduce_scatter | solution.py:68
  40.3 6.1 %collective-permute-start.1 = (bf16[256,128]{1,0:T(8,128)(2,1)S(1)}, bf16[256,128]{1,0:T(8,128)(2,1)S(1)}, u32[]{:S(2)}, u32[]{:S(2)}) collective-permute-start(bf16[256,128]{1,0:T(8,128)(2,1)S(1)} %collective-permute-done), channel_id=1, source_target_pairs={{0,4},{4,8},{8,12},{12,0},{1,5},{5,9},{9,13},{13,1},{2,6},{6,10},{... | collective-permute-start | bytes 196616 | tf_op jit(solution)/shard_map/ppermute | solution.py:20
  46.4 6.1 %collective-permute-start.2 = (bf16[256,128]{1,0:T(8,128)(2,1)S(1)}, bf16[256,128]{1,0:T(8,128)(2,1)S(1)}, u32[]{:S(2)}, u32[]{:S(2)}) collective-permute-start(bf16[256,128]{1,0:T(8,128)(2,1)S(1)} %collective-permute-done.1), channel_id=1, source_target_pairs={{0,4},{4,8},{8,12},{12,0},{1,5},{5,9},{9,13},{13,1},{2,6},{6,10},{... | collective-permute-start | bytes 196616 | tf_op jit(solution)/shard_map/ppermute | solution.py:20
  65.1 54.8 %all-reduce.2.cloned.1.call-start = ((), (), s32[]{:S(2)}) async-start(), calls=%async_computation.4 | async-start | bytes 262144 | tf_op jit(solution)/shard_map/psum | solution.py:69
Sparse Core Ops, SparseCore 0:
  65.2 22.7 reduce-scatter.1
  90.2 29.6 all-reduce.1
